TPU v7x, 256 devices: a whole 4x4x8 slice. The times are simulated.
256 devices in a mesh: vid: 8 (over z_hi, x), ta: 4 (over z_lo), ha: 8 (over y, core).
Axes of the slice: x: 4, y: 4, z: 8 (z_hi: 2, z_lo: 4; z = z_hi * 4 + z_lo), core: 2. Of those that a mesh axis runs over, the one named last changes fastest.
Arguments:
- queries: bfloat16 [128, 64, 16, 1536], P(('vid', 'ta'), 'ha'), parts along dimension 0, may hold values from -4.5 to 4.5
- keys: bfloat16 [128, 64, 16, 1536], P(('vid', 'ta'), 'ha'), parts along dimension 0, may hold values from -4.5 to 4.5
- values: bfloat16 [128, 64, 16, 1536], P(('vid', 'ta'), 'ha'), parts along dimension 0, may hold values from -6 to 6
- far_tiles: int32 [512, 12, 4], P(('vid', 'ta', 'ha')), parts along dimension 0, may hold values from 0 to 63, as said below
Outputs:
- attended: bfloat16 [128, 64, 16, 1536], P(('vid', 'ta'), 'ha'), parts along dimension 0
There are 8 independent parts, one for each index of `vid`. A program takes and returns all parts, laid end to end along the dimension named above; each array names one. Nothing has to cross between parts.
Inputs may be any that keep to these rules, and one draw needn't show every extreme that they name: `far_tiles`: every id names a tile of the same video. Among the 2 x 12 x 4 entries of one slab's query tiles, at most 4 name tiles of any one slab, and exactly 4 name tiles of some slab.
All inputs are finite; a program needn't handle non-finite values.
Results may differ from a plain program's by a relative error of at most 0.0059.
Values may be sent and summed in bfloat16 or wider, within the bound.
A program may use at most 192 MiB of HBM per device.

v0:
```python
import jax
import jax.numpy as jnp
from jax import lax
from jax.sharding import PartitionSpec as P

HEADS = 12
HD = 128
FAR = 4
TILE_W = 8
WIDTH = 16


def with_halo(array, sides, width):
    for axis, dim in sides:
        size, length = (lax.axis_size(axis), array.shape[dim])
        up = [(i, (i + 1) % size) for i in range(size - 1)]
        down = [(j, i) for i, j in up]
        last = lax.slice_in_dim(array, length - width, length, axis=dim)
        first = lax.slice_in_dim(array, 0, width, axis=dim)
        before = lax.ppermute(last, axis, up)
        after = lax.ppermute(first, axis, down)
        array = jnp.concatenate([before, array, after], axis=dim)
    return array


def to_tiles(block, tiles_w):
    frames, rows, cols, chans = block.shape
    shaped = block.reshape(frames, rows, tiles_w, cols // tiles_w, chans)
    return jnp.transpose(shaped, (2, 0, 1, 3, 4)).reshape(frames * rows * cols, chans)


def from_tiles(merged, shape, tiles_w):
    frames, rows, cols, chans = shape
    shaped = merged.reshape(tiles_w, frames, rows, cols // tiles_w, chans)
    return jnp.transpose(shaped, (1, 2, 0, 3, 4)).reshape(frames, rows, cols, chans)


def body(queries, keys, values, far_tiles):
    tiles_w = WIDTH // TILE_W
    tok = queries.shape[0] * queries.shape[1] * queries.shape[2]
    span = tok // tiles_w
    q_rows = to_tiles(queries, tiles_w)
    pair = jnp.stack((to_tiles(keys, tiles_w), to_tiles(values, tiles_w)), 0)[None, None]
    padded = with_halo(pair, (("ta", 0), ("ha", 1)), 1)
    window = jnp.concatenate(
        (pair[0, 0], padded[0, 1], padded[2, 1], padded[1, 0], padded[1, 2]), axis=1
    )
    t_index = lax.axis_index("ta")
    h_index = lax.axis_index("ha")
    present = jnp.stack(
        (
            jnp.array(True),
            t_index > 0,
            t_index < lax.axis_size("ta") - 1,
            h_index > 0,
            h_index < lax.axis_size("ha") - 1,
        )
    )
    key_mask = jnp.repeat(present, tok)
    owners = lax.axis_size(("ta", "ha"))
    items = far_tiles.reshape(-1)
    count = items.shape[0]
    capacity = (count + owners - 1) // owners + 1
    owner = items // tiles_w
    local = items % tiles_w
    head_ids = jnp.arange(count, dtype=jnp.int32) // FAR % HEADS
    code = local * HEADS + head_ids
    onehot = (owner[:, None] == jnp.arange(owners, dtype=jnp.int32)[None, :]).astype(jnp.int32)
    rank = jnp.sum((jnp.cumsum(onehot, 0) - 1) * onehot, 1)
    slot = owner * capacity + rank
    request = (
        jnp.full((owners * capacity,), -1, jnp.int32).at[slot].set(code).reshape(owners, capacity)
    )
    asked = lax.all_to_all(request, ("ta", "ha"), split_axis=0, concat_axis=0, tiled=True)
    table = pair.reshape(2, tiles_w, span, HEADS, HD)
    table = jnp.transpose(table, (1, 3, 0, 2, 4)).reshape(tiles_w * HEADS, 2, span, HD)
    reply = table[jnp.clip(asked, 0, tiles_w * HEADS - 1)]
    back = lax.all_to_all(reply, ("ta", "ha"), split_axis=0, concat_axis=0, tiled=True)
    fetched = back.reshape((owners * capacity,) + back.shape[2:])[slot]
    fetched = fetched.reshape(tiles_w, HEADS, FAR, 2, span, HD)
    scale = HD ** (-0.5)

    def one_head(head):
        start = head * HD
        q_head = lax.dynamic_slice_in_dim(q_rows, start, HD, 1)
        k_near = lax.dynamic_slice_in_dim(window[0], start, HD, 1)
        v_near = lax.dynamic_slice_in_dim(window[1], start, HD, 1)
        far_head = lax.dynamic_index_in_dim(fetched, head, 1, keepdims=False)
        k_far = far_head[:, :, 0].reshape(tiles_w, FAR * span, HD)
        v_far = far_head[:, :, 1].reshape(tiles_w, FAR * span, HD)
        near = jnp.einsum("qd,kd->qk", q_head, k_near, preferred_element_type=jnp.float32) * scale
        near = jnp.where(key_mask[None, :], near, -1e30)
        q_split = q_head.reshape(tiles_w, span, HD)
        distant = (
            jnp.einsum("tqd,tkd->tqk", q_split, k_far, preferred_element_type=jnp.float32) * scale
        )
        top = jnp.maximum(jnp.max(near, 1), jnp.max(distant, 2).reshape(-1))
        p_near = jnp.exp(near - top[:, None]).astype(jnp.bfloat16)
        p_far = jnp.exp(distant - top.reshape(tiles_w, span, 1)).astype(jnp.bfloat16)
        total = jnp.sum(p_near.astype(jnp.float32), 1) + jnp.sum(
            p_far.astype(jnp.float32), 2
        ).reshape(-1)
        accum = jnp.dot(p_near, v_near, preferred_element_type=jnp.float32)
        accum = accum + jnp.einsum(
            "tqk,tkd->tqd", p_far, v_far, preferred_element_type=jnp.float32
        ).reshape(tok, HD)
        return (accum / total[:, None]).astype(jnp.bfloat16)

    per_head = lax.map(one_head, jnp.arange(HEADS, dtype=jnp.int32))
    merged = jnp.transpose(per_head, (1, 0, 2)).reshape(tok, HEADS * HD)
    return from_tiles(merged, queries.shape, tiles_w)


def solution(mesh):
    in_specs = (
        P(("vid", "ta"), "ha", None, None),
        P(("vid", "ta"), "ha", None, None),
        P(("vid", "ta"), "ha", None, None),
        P(("vid", "ta", "ha"), None, None),
    )
    out_specs = P(("vid", "ta"), "ha", None, None)
    return jax.shard_map(body, mesh=mesh, in_specs=in_specs, out_specs=out_specs, check_vma=False)
```

profile of v0, /device:TPU:67, one launch (start us, length us, event | category | flops | bytes accessed | tf_op | source)
XLA Modules:
  0.0 1001.8 jit_solution(18132290197444670434)
XLA Ops:
  3.1 8.7 all-to-all-start
  15.1 4.0 stack.31
  19.0 4.0 stack.30
  23.0 3.0 maximum_bitcast_fusion
  28.8 10.1 %gather_fusion = bf16[128,2,256,128]{3,2,1,0:T(8,128)(2,1)} fusion(bf16[24,2,256,128]{3,2,1,0:T(8,128)(2,1)} %bitcast.124, s32[1024]{0:T(1024)S(1)} %pad_clamp_fusion.1), kind=kCustom, calls=%fused_computation | custom fusion | bytes 33554944 | tf_op jit(solution)/shard_map/gather | solution.py:77
  38.9 7.8 all-to-all-start.1
  48.8 3.2 collective-permute-start
  54.3 435.2 %collective-permute-done = bf16[1,1,2,512,1536]{4,3,2,1,0:T(8,128)(2,1)S(1)} collective-permute-done((bf16[1,1,2,512,1536]{4,3,2,1,0:T(8,128)(2,1)S(1)}, bf16[1,1,2,512,1536]{4,3,2,1,0:T(8,128)(2,1)S(1)}, u32[]{:S(2)}, u32[]{:S(2)}) %collective-permute-start) | collective-permute-done | bytes 3145760 | tf_op jit(solution)/shard_map/ppermute | solution.py:20
  489.4 5.4 pad_maximum_fusion
  496.8 6.2 collective-permute-start.3
  504.5 4.0 bitcast_dynamic-update-slice_fusion.1
  510.4 88.4 %collective-permute-done.2 = bf16[3,1,2,512,1536]{4,3,2,1,0:T(8,128)(2,1)} collective-permute-done((bf16[3,1,2,512,1536]{4,3,2,1,0:T(8,128)(2,1)}, bf16[3,1,2,512,1536]{4,3,2,1,0:T(8,128)(2,1)}, u32[]{:S(2)}, u32[]{:S(2)}) %collective-permute-start.2) | collective-permute-done | bytes 9437216 | tf_op jit(solution)/shard_map/ppermute | solution.py:20
  598.7 3.7 fusion.15
  603.1 3.7 fusion.14
  606.9 12.6 %gather_fusion.1 = bf16[96,2,256,128]{3,2,1,0:T(8,128)(2,1)} fusion(bf16[128,2,256,128]{3,2,1,0:T(8,128)(2,1)} %bitcast.21, s32[1024]{0:T(1024)S(1)} %pad_clamp_fusion), kind=kCustom, calls=%fused_computation.1 | custom fusion | bytes 25166208 | tf_op jit(solution)/shard_map/gather | solution.py:79
  619.5 374.0 %while.11 = (s32[]{:T(128)}, bf16[12,512,128]{2,1,0:T(8,128)(2,1)}, s32[12]{0:T(128)S(1)}, bf16[512,1536]{1,0:T(8,128)(2,1)}, bf16[2,2560,1536]{2,1,0:T(8,128)(2...) while((s32[]{:T(128)}, bf16[12,512,128]{2,1,0:T(8,128)(2,1)}, ...), condition=%wide.region_8.9_spmd.clone, body=%wide.region_3.8_spmd.clone.sunk | while | flops 954138112 | bytes 69657864 | solution.py:109
  626.3 10.9 %fusion.51 = (bf16[1,2560,1536]{2,1,0:T(8,128)(2,1)}, bf16[1,2560,1536]{2,1,0:T(8,128)(2,1)}) fusion(bf16[2,2560,1536]{2,1,0:T(8,128)(2,1)} %get-tuple-element.211), kind=kLoop, calls=%fused_computation.68.clone.1 | loop fusion | bytes 31457280 | tf_op jit(solution)/shard_map/while/body/eval_jaxpr/slice | solution.py:87
  637.3 4.4 fusion.52
  643.9 3.5 convert_reduce_fusion.4
  648.0 2.6 fusion.54
  657.5 10.9 %fusion.51 = (bf16[1,2560,1536]{2,1,0:T(8,128)(2,1)}, bf16[1,2560,1536]{2,1,0:T(8,128)(2,1)}) fusion(bf16[2,2560,1536]{2,1,0:T(8,128)(2,1)} %get-tuple-element.211), kind=kLoop, calls=%fused_computation.68.clone.1 | loop fusion | bytes 31457280 | tf_op jit(solution)/shard_map/while/body/eval_jaxpr/slice | solution.py:87
  668.5 4.4 fusion.52
  675.1 3.5 convert_reduce_fusion.4
  679.2 2.6 fusion.54
  688.7 10.9 %fusion.51 = (bf16[1,2560,1536]{2,1,0:T(8,128)(2,1)}, bf16[1,2560,1536]{2,1,0:T(8,128)(2,1)}) fusion(bf16[2,2560,1536]{2,1,0:T(8,128)(2,1)} %get-tuple-element.211), kind=kLoop, calls=%fused_computation.68.clone.1 | loop fusion | bytes 31457280 | tf_op jit(solution)/shard_map/while/body/eval_jaxpr/slice | solution.py:87
  699.6 4.4 fusion.52
  706.3 3.5 convert_reduce_fusion.4
  710.4 2.6 fusion.54
  719.8 10.9 %fusion.51 = (bf16[1,2560,1536]{2,1,0:T(8,128)(2,1)}, bf16[1,2560,1536]{2,1,0:T(8,128)(2,1)}) fusion(bf16[2,2560,1536]{2,1,0:T(8,128)(2,1)} %get-tuple-element.211), kind=kLoop, calls=%fused_computation.68.clone.1 | loop fusion | bytes 31457280 | tf_op jit(solution)/shard_map/while/body/eval_jaxpr/slice | solution.py:87
  730.8 4.4 fusion.52
  737.4 3.5 convert_reduce_fusion.4
  741.5 2.6 fusion.54
  751.0 10.9 %fusion.51 = (bf16[1,2560,1536]{2,1,0:T(8,128)(2,1)}, bf16[1,2560,1536]{2,1,0:T(8,128)(2,1)}) fusion(bf16[2,2560,1536]{2,1,0:T(8,128)(2,1)} %get-tuple-element.211), kind=kLoop, calls=%fused_computation.68.clone.1 | loop fusion | bytes 31457280 | tf_op jit(solution)/shard_map/while/body/eval_jaxpr/slice | solution.py:87
  762.0 4.4 fusion.52
  768.6 3.5 convert_reduce_fusion.4
  772.7 2.6 fusion.54
  782.2 10.9 %fusion.51 = (bf16[1,2560,1536]{2,1,0:T(8,128)(2,1)}, bf16[1,2560,1536]{2,1,0:T(8,128)(2,1)}) fusion(bf16[2,2560,1536]{2,1,0:T(8,128)(2,1)} %get-tuple-element.211), kind=kLoop, calls=%fused_computation.68.clone.1 | loop fusion | bytes 31457280 | tf_op jit(solution)/shard_map/while/body/eval_jaxpr/slice | solution.py:87
  793.1 4.4 fusion.52
  799.8 3.5 convert_reduce_fusion.4
  803.9 2.6 fusion.54
  813.3 10.9 %fusion.51 = (bf16[1,2560,1536]{2,1,0:T(8,128)(2,1)}, bf16[1,2560,1536]{2,1,0:T(8,128)(2,1)}) fusion(bf16[2,2560,1536]{2,1,0:T(8,128)(2,1)} %get-tuple-element.211), kind=kLoop, calls=%fused_computation.68.clone.1 | loop fusion | bytes 31457280 | tf_op jit(solution)/shard_map/while/body/eval_jaxpr/slice | solution.py:87
  824.3 4.4 fusion.52
  830.9 3.5 convert_reduce_fusion.4
  835.0 2.6 fusion.54
  844.5 10.9 %fusion.51 = (bf16[1,2560,1536]{2,1,0:T(8,128)(2,1)}, bf16[1,2560,1536]{2,1,0:T(8,128)(2,1)}) fusion(bf16[2,2560,1536]{2,1,0:T(8,128)(2,1)} %get-tuple-element.211), kind=kLoop, calls=%fused_computation.68.clone.1 | loop fusion | bytes 31457280 | tf_op jit(solution)/shard_map/while/body/eval_jaxpr/slice | solution.py:87
  855.5 4.4 fusion.52
  862.1 3.5 convert_reduce_fusion.4
  866.2 2.6 fusion.54
  875.7 10.9 %fusion.51 = (bf16[1,2560,1536]{2,1,0:T(8,128)(2,1)}, bf16[1,2560,1536]{2,1,0:T(8,128)(2,1)}) fusion(bf16[2,2560,1536]{2,1,0:T(8,128)(2,1)} %get-tuple-element.211), kind=kLoop, calls=%fused_computation.68.clone.1 | loop fusion | bytes 31457280 | tf_op jit(solution)/shard_map/while/body/eval_jaxpr/slice | solution.py:87
  886.6 4.4 fusion.52
  893.3 3.5 convert_reduce_fusion.4
  897.3 2.6 fusion.54
  906.8 10.9 %fusion.51 = (bf16[1,2560,1536]{2,1,0:T(8,128)(2,1)}, bf16[1,2560,1536]{2,1,0:T(8,128)(2,1)}) fusion(bf16[2,2560,1536]{2,1,0:T(8,128)(2,1)} %get-tuple-element.211), kind=kLoop, calls=%fused_computation.68.clone.1 | loop fusion | bytes 31457280 | tf_op jit(solution)/shard_map/while/body/eval_jaxpr/slice | solution.py:87
  917.8 4.4 fusion.52
  924.4 3.5 convert_reduce_fusion.4
  938.0 10.9 %fusion.51 = (bf16[1,2560,1536]{2,1,0:T(8,128)(2,1)}, bf16[1,2560,1536]{2,1,0:T(8,128)(2,1)}) fusion(bf16[2,2560,1536]{2,1,0:T(8,128)(2,1)} %get-tuple-element.211), kind=kLoop, calls=%fused_computation.68.clone.1 | loop fusion | bytes 31457280 | tf_op jit(solution)/shard_map/while/body/eval_jaxpr/slice | solution.py:87
  949.0 4.4 fusion.52
  955.6 3.5 convert_reduce_fusion.4
  969.2 10.9 %fusion.51 = (bf16[1,2560,1536]{2,1,0:T(8,128)(2,1)}, bf16[1,2560,1536]{2,1,0:T(8,128)(2,1)}) fusion(bf16[2,2560,1536]{2,1,0:T(8,128)(2,1)} %get-tuple-element.211), kind=kLoop, calls=%fused_computation.68.clone.1 | loop fusion | bytes 31457280 | tf_op jit(solution)/shard_map/while/body/eval_jaxpr/slice | solution.py:87
  980.1 4.4 fusion.52
  986.8 3.5 convert_reduce_fusion.4
  990.8 2.6 fusion.54
  993.5 4.0 copy.55
  997.4 3.0 reshape_reshape.3
  (252 shorter events, 115.1 us)
Async XLA Ops:
  0.0 11.8 %copy-start = (bf16[4,8,16,1536]{3,2,1,0:T(8,128)(2,1)S(1)}, bf16[4,8,16,1536]{3,2,1,0:T(8,128)(2,1)}, u32[]{:S(2)}) copy-start(bf16[4,8,16,1536]{3,2,1,0:T(8,128)(2,1)} %param.8) | copy-start | bytes 4718596
  3.1 25.4 %all-to-all-start = ((s32[32,1,4]{2,1,0:T(1,128)}), s32[32,1,4]{2,1,0:T(1,128)S(1)}, u32[]{:S(2)}, u32[]{:S(2)}) async-start(s32[32,1,4]{2,1,0:T(1,128)} %bitcast.18), calls=%async_computation | async-start | bytes 32768 | tf_op jit(solution)/shard_map/all_to_all | solution.py:74
  11.8 1.8 copy-start.7
  38.9 567.9 %all-to-all-start.1 = ((bf16[32,4,2,256,128]{4,3,2,1,0:T(8,128)(2,1)}), bf16[32,4,2,256,128]{4,3,2,1,0:T(8,128)(2,1)}, u32[]{:S(2)}, u32[]{:S(2)}) async-start(bf16[32,4,2,256,128]{4,3,2,1,0:T(8,128)(2,1)} %bitcast.125), calls=%async_computation.1 | async-start | bytes 33554432 | tf_op jit(solution)/shard_map/all_to_all | solution.py:78
  48.8 454.2 %copy-start.6 = (bf16[4,8,16,1536]{3,2,1,0:T(8,128)(2,1)S(1)}, bf16[4,8,16,1536]{3,2,1,0:T(8,128)(2,1)}, u32[]{:S(2)}) copy-start(bf16[4,8,16,1536]{3,2,1,0:T(8,128)(2,1)} %param.6) | copy-start | bytes 4718596
  48.8 440.6 %collective-permute-start = (bf16[1,1,2,512,1536]{4,3,2,1,0:T(8,128)(2,1)S(1)}, bf16[1,1,2,512,1536]{4,3,2,1,0:T(8,128)(2,1)S(1)}, u32[]{:S(2)}, u32[]{:S(2)}) collective-permute-start(bf16[1,1,2,512,1536]{4,3,2,1,0:T(8,128)(2,1)S(1)} %get-tuple-element.112), channel_id=1, source_target_pairs={{0,8},{8,16},{16,24},{1,9},{9,17},{17,25},{2,10},{10,18},{18,26},{... | collective-permute-start | bytes 9437192 | tf_op jit(solution)/shard_map/ppermute | solution.py:20
  52.1 437.4 %collective-permute-start.1 = (bf16[1,1,2,512,1536]{4,3,2,1,0:T(8,128)(2,1)S(1)}, bf16[1,1,2,512,1536]{4,3,2,1,0:T(8,128)(2,1)S(1)}, u32[]{:S(2)}, u32[]{:S(2)}) collective-permute-start(bf16[1,1,2,512,1536]{4,3,2,1,0:T(8,128)(2,1)S(1)} %get-tuple-element.112), channel_id=1, source_target_pairs={{8,0},{16,8},{24,16},{9,1},{17,9},{25,17},{10,2},{18,10},{26,18},{... | collective-permute-start | bytes 9437192 | tf_op jit(solution)/shard_map/ppermute | solution.py:21
  489.4 5.5 copy-start.3
  489.4 5.4 copy-start.4
  494.9 103.8 %collective-permute-start.2 = (bf16[3,1,2,512,1536]{4,3,2,1,0:T(8,128)(2,1)}, bf16[3,1,2,512,1536]{4,3,2,1,0:T(8,128)(2,1)}, u32[]{:S(2)}, u32[]{:S(2)}) collective-permute-start(bf16[3,1,2,512,1536]{4,3,2,1,0:T(8,128)(2,1)} %pad_maximum_fusion), channel_id=1, source_target_pairs={{0,1},{1,2},{2,3},{3,4},{4,5},{5,6},{6,7},{8,9},{9,10},{10,11},{11... | collective-permute-start | bytes 28311560 | tf_op jit(solution)/shard_map/ppermute | solution.py:20
  496.8 106.3 %collective-permute-start.3 = (bf16[3,1,2,512,1536]{4,3,2,1,0:T(8,128)(2,1)}, bf16[3,1,2,512,1536]{4,3,2,1,0:T(8,128)(2,1)}, u32[]{:S(2)}, u32[]{:S(2)}) collective-permute-start(bf16[3,1,2,512,1536]{4,3,2,1,0:T(8,128)(2,1)} %pad_maximum_fusion), channel_id=1, source_target_pairs={{1,0},{2,1},{3,2},{4,3},{5,4},{6,5},{7,6},{9,8},{10,9},{11,10},{12... | collective-permute-start | bytes 28311560 | tf_op jit(solution)/shard_map/ppermute | solution.py:21
  504.5 4.0 copy-start.5
  643.9 3.6 copy-start.2
  675.1 3.6 copy-start.2
  706.3 3.6 copy-start.2
  737.4 3.6 copy-start.2
  768.6 3.6 copy-start.2
  799.8 3.6 copy-start.2
  830.9 3.6 copy-start.2
  862.1 3.6 copy-start.2
  893.3 3.6 copy-start.2
  924.4 3.6 copy-start.2
  955.6 3.6 copy-start.2
  986.8 3.6 copy-start.2
  993.5 8.3 copy-start.1
where the time goes:
time: 1000 us
  waiting for transfers between devices  524 us (52%)
  local copies, waits for them, and re-layouts  229 us (23%)
  matrix products  132 us (13%)
  other arithmetic  59.8 us (6%)
  starting transfers between devices  30 us (3%)
  loops' own time  27.3 us (3%)
    ppermute x2, waiting for transfers between devices, with_halo(): before = lax.ppermute(last, axis, up)  524 us
    slice x12, local copies, waits for them, and re-layouts, one_head(): v_near = lax.dynamic_slice_in_dim(window[1], start, HD, 1)  130 us
    dot_general x12, matrix products, one_head(): jnp.einsum('qd,kd->qk', q_head, k_near, preferred_element_type=jnp.float32)  53 us
    reduce_sum x12, other arithmetic, one_head(): jnp.sum(p_near.astype(jnp.float32), 1)  42.5 us
    dot_general x12, matrix products, one_head(): accum = jnp.dot(p_near, v_near, preferred_element_type=jnp.float32)  31.5 us
    another operation x1, loops' own time, body(): per_head = lax.map(one_head, jnp.arange(HEADS, dtype=jnp.int32))  27.3 us
    dot_general x12, matrix products, one_head(): jnp.einsum('tqk,tkd->tqd', p_far, v_far, preferred_element_type=jnp.float32)  25.8 us
    dot_general x12, matrix products, one_head(): jnp.einsum('tqd,tkd->tqk', q_split, k_far, preferred_element_type=jnp.flo...  21.2 us
  transfers between devices with their start and end apart: 6, of which 3 were waited for; matrix products, arithmetic and copies ran while one was open for 4% of the time, Pallas kernels for 0%

commit v1 on v0

v1 whole, which is shorter than its diff:
```python
import functools

import jax
import jax.numpy as jnp
from jax import lax
from jax.experimental import pallas as pl
from jax.experimental.pallas import tpu as pltpu
from jax.sharding import PartitionSpec as P

HEADS = 12
HD = 128
FAR = 4
NT = 4
NH = 8
NY = 4
GROUP = HEADS // NT
TILE = 256
SLAB = 512
KEYS = 5 * SLAB + FAR * TILE
EXP2_SCALE = HD**-0.5 * 1.4426950408889634
MASKED = -1e30
MESH = pl.DeviceIdType.MESH

STEPS = (
    ("C", 0, 1), ("D", 0, 0), ("C", 0, 2), ("D", 0, 1), ("C", 1, 1), ("C", 0, 3), ("D", 0, 2), ("E", 0, 0),
    ("D", 1, 0), ("C", 1, 2), ("D", 0, 3), ("E", 0, 1), ("D", 1, 1), ("C", 2, 1), ("C", 1, 3), ("E", 0, 2),
    ("D", 1, 2), ("D", 2, 0), ("C", 2, 2), ("E", 0, 3), ("E", 1, 0), ("C", 2, 3), ("Q", 0, 0), ("E", 1, 1),
    ("D", 1, 3), ("X", 0, 0), ("D", 2, 1), ("E", 1, 2), ("D", 2, 2), ("E", 1, 3), ("X", 1, 0),
    ("D", 2, 3), ("E", 2, 0), ("E", 2, 1), ("E", 2, 2), ("E", 2, 3), ("X", 2, 0), ("W", 0, 0), ("W", 1, 0), ("W", 2, 0),
)


def untile(block):
    x = block.astype(jnp.float32).reshape(32, 2, 8, HD)
    return [x[:, w].reshape(TILE, HD).astype(jnp.bfloat16) for w in range(2)]


def kernel(
    q_hbm, k_hbm, v_hbm, far_in, out_hbm,
    out, q_in, k_in, v_in, kv_out, q_out, t0, t1, t2, q_all, o_out, o_in, far_all, scores,
    load_sem, own_sem, out_sem, far_s, far_r, z_s, z_r, q_s, q_r, o_s, o_r, y_s, y_r,
):
    tables = (t0, t1, t2)
    z = lax.axis_index("ta")
    h = lax.axis_index("ha")
    y = h // 2
    c = h - 2 * y
    h_after = lax.rem(y + 1, NY) * 2 + c
    h_before = lax.rem(y + NY - 1, NY) * 2 + c
    h_across = lax.rem(y + 2, NY) * 2 + c
    h_twin = 2 * y + 1 - c

    def remote(src, dst, send, recv, device):
        return pltpu.make_async_remote_copy(
            src_ref=src, dst_ref=dst, send_sem=send, recv_sem=recv, device_id=device, device_id_type=MESH
        )

    loads = [
        pltpu.make_async_copy(src, dst, load_sem.at[i])
        for i, (src, dst) in enumerate(((k_hbm, k_in), (v_hbm, v_in), (q_hbm, q_in)))
    ]
    for load in loads:
        load.start()

    barrier = pltpu.get_barrier_semaphore()
    partners = [{"ta": lax.rem(z + k, NT)} for k in range(1, NT)]
    partners += [{"ha": h_after}, {"ha": h_before}, {"ha": h_twin}]
    for partner in partners:
        pl.semaphore_signal(barrier, inc=1, device_id=partner, device_id_type=MESH)

    def to(k):
        return lax.rem(z + k, NT)

    def came(k):
        return lax.rem(z + NT - k, NT)

    def far_copy(k):
        return remote(far_in, far_all.at[z], far_s.at[k], far_r.at[k], {"ta": to(k)})

    def kv_copy(j, k):
        return remote(
            kv_out.at[to(k) * GROUP + j], tables[j].at[z * NH + h], z_s.at[j, k], z_r.at[j, k], {"ta": to(k)}
        )

    def q_copy(j, k):
        return remote(q_out.at[to(k) * GROUP + j], q_all.at[j, z], q_s.at[j, k], q_r.at[j, k], {"ta": to(k)})

    def o_copy(j, k):
        return remote(o_out.at[j, to(k)], o_in.at[z * GROUP + j], o_s.at[j, k], o_r.at[j, k], {"ta": to(k)})

    def y_copy(j, k, i):
        table = tables[j]
        base = came(k) * NH

        def slab(row):
            return table.at[base + row]

        if i < 3:
            src = kv_out.at[z * GROUP + j] if k == 0 else slab(h)
            dst = slab(h)
            device = (h_after, h_before, h_twin)[i]
        elif i == 3:
            src = dst = table.at[base + h_before, 0]
            device = h_after
        elif i == 4:
            src = dst = table.at[base + h_after, 1]
            device = h_before
        else:
            src = dst = slab((h_before, h_after, h_across)[i - 5])
            device = h_twin
        return remote(src, dst, y_s.at[j, k, i], y_r.at[j, k, i], {"ha": device})

    def own_kv(j):
        return pltpu.make_async_copy(kv_out.at[z * GROUP + j], tables[j].at[z * NH + h], own_sem.at[j, 0])

    def own_q(j):
        return pltpu.make_async_copy(q_out.at[z * GROUP + j], q_all.at[j, z], own_sem.at[j, 1])

    def own_o(j):
        return pltpu.make_async_copy(o_out.at[j, z], o_in.at[z * GROUP + j], own_sem.at[j, 2])

    own_far = pltpu.make_async_copy(far_in, far_all.at[z], own_sem.at[0, 3])

    def lanes(head):
        return pl.ds(pl.multiple_of(head * HD, HD), HD)

    own_far.start()
    loads[0].wait()
    loads[1].wait()
    for j in range(GROUP):
        for k in range(NT):
            head = to(k) * GROUP + j
            for i, source in enumerate((k_in, v_in)):
                for w, tile in enumerate(untile(source[:, :, :, lanes(head)])):
                    kv_out[head, i, w] = tile
        if j == 0:
            pl.semaphore_wait(barrier, len(partners))
        for k in range(1, NT):
            kv_copy(j, k).start()
        for i in range(3):
            y_copy(j, 0, i).start()
        own_kv(j).start()
    for k in range(1, NT):
        far_copy(k).start()
    loads[2].wait()
    for j in range(GROUP):
        for k in range(NT):
            head = to(k) * GROUP + j
            for w, tile in enumerate(untile(q_in[:, :, :, lanes(head)])):
                q_out[head, w] = tile
        own_q(j).start()

    def send_queries():
        for j in range(GROUP):
            for k in range(1, NT):
                q_copy(j, k).start()

    at_end = jnp.logical_or(z == 0, z == NT - 1)
    pl.when(jnp.logical_not(at_end))(send_queries)

    def step_d(j, k):
        y_copy(j, k, 0).wait_recv()
        y_copy(j, k, 3).start()
        y_copy(j, k, 5).start()
        y_copy(j, k, 1).wait_recv()
        y_copy(j, k, 4).start()
        y_copy(j, k, 6).start()

    def step_e(j, k):
        y_copy(j, k, 3).wait_recv()
        y_copy(j, k, 4).wait_recv()
        y_copy(j, k, 7).start()

    def unit(j, t, w):
        table = tables[j]
        q = q_all[j, t, w]
        near = (
            (t, h, None),
            (jnp.maximum(t - 1, 0), h, t > 0),
            (jnp.minimum(t + 1, NT - 1), h, t < NT - 1),
            (t, jnp.maximum(h - 1, 0), h > 0),
            (t, jnp.minimum(h + 1, NH - 1), h < NH - 1),
        )
        ids = [far_all[t, w, f, z * GROUP + j] for f in range(FAR)]
        contract = (((1,), (1,)), ((), ()))
        high = None

        def score(keys, start, bias, high):
            s = lax.dot_general(q, keys, contract, preferred_element_type=jnp.float32)
            if bias is not None:
                s = s + bias
            scores[w, :, start : start + keys.shape[0]] = s
            for at in range(0, keys.shape[0], HD):
                part = s[:, at : at + HD]
                high = part if high is None else jnp.maximum(high, part)
            return high

        for n, (tt, hh, there) in enumerate(near):
            keys = table[tt * NH + hh, 0].reshape(SLAB, HD)
            bias = None if there is None else jnp.where(there, 0.0, MASKED).astype(jnp.float32)
            high = score(keys, n * SLAB, bias, high)
        for f, tile in enumerate(ids):
            high = score(table[tile // 2, 0, lax.rem(tile, 2)], 5 * SLAB + f * TILE, None, high)
        top = jnp.max(high, axis=1, keepdims=True)
        accum = jnp.zeros((TILE, 2 * HD), jnp.float32)

        def gather(values, start, accum):
            s = scores[w, :, start : start + values.shape[0]]
            p = jnp.exp2((s - top) * EXP2_SCALE).astype(jnp.bfloat16)
            wide = jnp.concatenate((values, jnp.ones_like(values)), axis=1)
            return accum + jnp.dot(p, wide, preferred_element_type=jnp.float32)

        for n, (tt, hh, _) in enumerate(near):
            accum = gather(table[tt * NH + hh, 1].reshape(SLAB, HD), n * SLAB, accum)
        for f, tile in enumerate(ids):
            accum = gather(table[tile // 2, 1, lax.rem(tile, 2)], 5 * SLAB + f * TILE, accum)
        o_out[j, t, w] = (accum[:, :HD] / accum[:, HD:]).astype(jnp.bfloat16)

    def attend(j):
        if j == 0:
            own_far.wait()
            for k in range(1, NT):
                far_copy(k).wait_recv()
        own_kv(j).wait()
        own_q(j).wait()
        for k in range(1, NT):
            q_copy(j, k).wait_recv()
        for k in range(NT):
            for i in (2, 5, 6, 7):
                y_copy(j, k, i).wait_recv()

        def queries_of(k, carry):
            t = to(k)
            for w in range(2):
                unit(j, t, w)

            @pl.when(k < NT)
            def _():
                o_copy(j, k).start()

            return carry

        lax.fori_loop(1, NT + 1, queries_of, 0)
        own_o(j).start()

    def write(j, k):
        head = came(k) * GROUP + j
        return pltpu.make_async_copy(out.at[:, :, :, lanes(head)], out_hbm.at[:, :, :, lanes(head)], out_sem.at[j, k])

    def collect(j):
        own_o(j).wait()
        for k in range(NT):
            if k:
                o_copy(j, k).wait_recv()
            head = came(k) * GROUP + j
            x = [o_in[head, w].astype(jnp.float32).reshape(32, 8, HD) for w in range(2)]
            out[:, :, :, lanes(head)] = (
                jnp.concatenate(x, axis=1).astype(jnp.bfloat16).reshape(4, 8, 16, HD)
            )
            write(j, k).start()

    for step, j, k in STEPS:
        if step == "C":
            kv_copy(j, k).wait_recv()
            for i in range(3):
                y_copy(j, k, i).start()
        elif step == "D":
            step_d(j, k)
        elif step == "E":
            step_e(j, k)
        elif step == "Q":
            pl.when(at_end)(send_queries)
        elif step == "X":
            attend(j)
        else:
            collect(j)

    for k in range(1, NT):
        far_copy(k).wait_send()
    for j in range(GROUP):
        for k in range(NT):
            if k:
                kv_copy(j, k).wait_send()
                q_copy(j, k).wait_send()
                o_copy(j, k).wait_send()
            for i in range(8):
                y_copy(j, k, i).wait_send()
            write(j, k).wait()


def body(queries, keys, values, far_tiles):
    bf = jnp.bfloat16
    far_tiles = jnp.transpose(far_tiles, (0, 2, 1))
    any_space = pl.BlockSpec(memory_space=pl.ANY)
    dma = pltpu.SemaphoreType.DMA
    table = pltpu.VMEM((NT * NH, 2, 2, TILE, HD), bf)
    slab = pltpu.VMEM(queries.shape, bf)
    return pl.pallas_call(
        kernel,
        out_shape=jax.ShapeDtypeStruct(queries.shape, bf),
        in_specs=[any_space] * 3 + [pl.BlockSpec(memory_space=pltpu.SMEM)],
        out_specs=any_space,
        scratch_shapes=[
            slab, slab, slab, slab,
            pltpu.VMEM((HEADS, 2, 2, TILE, HD), bf),
            pltpu.VMEM((HEADS, 2, TILE, HD), bf),
            table, table, table,
            pltpu.VMEM((GROUP, NT, 2, TILE, HD), bf),
            pltpu.VMEM((GROUP, NT, 2, TILE, HD), bf),
            pltpu.VMEM((HEADS, 2, TILE, HD), bf),
            pltpu.SMEM((NT,) + far_tiles.shape, jnp.int32),
            pltpu.VMEM((2, TILE, KEYS), jnp.float32),
            dma((3,)), dma((GROUP, 4)), dma((GROUP, NT)), dma((NT,)), dma((NT,)),
            dma((GROUP, NT)), dma((GROUP, NT)), dma((GROUP, NT)), dma((GROUP, NT)), dma((GROUP, NT)), dma((GROUP, NT)),
            dma((GROUP, NT, 8)), dma((GROUP, NT, 8)),
        ],
        compiler_params=pltpu.CompilerParams(
            collective_id=0, has_side_effects=True, vmem_limit_bytes=60 << 20
        ),
    )(queries, keys, values, far_tiles)


def solution(mesh):
    spec = P(("vid", "ta"), "ha", None, None)
    in_specs = (spec, spec, spec, P(("vid", "ta", "ha"), None, None))
    return jax.shard_map(body, mesh=mesh, in_specs=in_specs, out_specs=spec, check_vma=False)
```

time: 1000 us -> 154 us (0.15)
  the two profiles are of different devices: /device:TPU:67 before, /device:TPU:36 now
where the time goes in v1:
time: 154 us
  Pallas kernels  151 us (98%)
  local copies, waits for them, and re-layouts  2.65 us (2%)
    pallas_call x1, Pallas kernels, body(): pl.pallas_call(kernel, out_shape=jax.ShapeDtypeStruct(queries.shape, bf),...  151 us

profile of v1, /device:TPU:36, one launch (start us, length us, event | category | flops | bytes accessed | tf_op | source)
XLA Modules:
  0.0 153.8 jit_solution(8921929574835691498)
XLA Ops:
  0.0 151.1 %shard_map.46 = bf16[4,8,16,1536]{3,2,1,0:T(8,128)(2,1)} custom-call(bf16[4,8,16,1536]{3,2,1,0:T(8,128)(2,1)} %q_hbm.1, bf16[4,8,16,1536]{3,2,1,0:T(8,128)(2,1)} %k_hbm.1, bf16[4,8,16,1536]{3,2,1,0:T(8,128)(2,1)} %v_hbm.1, s32[2,4,12]{2,1,0:T(4,128)} %bitcast.1), custom_call_target="tpu_custom_call" | custom-call | tf_op jit(solution)/shard_map/pallas_call | solution.py:298
  151.1 2.7 %copy.6 = bf16[4,8,16,1536]{3,2,1,0:T(8,128)(2,1)} copy(bf16[4,8,16,1536]{3,2,1,0:T(8,128)(2,1)} %shard_map.46) | data formatting | bytes 3145728

commit v2 on v1

--- a/solution.py
+++ b/solution.py
@@ -22,11 +22,12 @@
 MESH = pl.DeviceIdType.MESH
 
 STEPS = (
-    ("C", 0, 1), ("D", 0, 0), ("C", 0, 2), ("D", 0, 1), ("C", 1, 1), ("C", 0, 3), ("D", 0, 2), ("E", 0, 0),
-    ("D", 1, 0), ("C", 1, 2), ("D", 0, 3), ("E", 0, 1), ("D", 1, 1), ("C", 2, 1), ("C", 1, 3), ("E", 0, 2),
-    ("D", 1, 2), ("D", 2, 0), ("C", 2, 2), ("E", 0, 3), ("E", 1, 0), ("C", 2, 3), ("Q", 0, 0), ("E", 1, 1),
-    ("D", 1, 3), ("X", 0, 0), ("D", 2, 1), ("E", 1, 2), ("D", 2, 2), ("E", 1, 3), ("X", 1, 0),
-    ("D", 2, 3), ("E", 2, 0), ("E", 2, 1), ("E", 2, 2), ("E", 2, 3), ("X", 2, 0), ("W", 0, 0), ("W", 1, 0), ("W", 2, 0),
+    ("C", 0, 1), ("D", 0, 0), ("C", 0, 2), ("D", 1, 0), ("C", 2, 0), ("E", 0, 0), ("D", 0, 1), ("E", 1, 0),
+    ("D", 0, 2), ("E", 0, 1), ("C", 1, 1), ("C", 0, 3), ("C", 1, 2), ("D", 2, 0), ("E", 0, 2), ("D", 1, 1),
+    ("E", 2, 0), ("C", 2, 1), ("D", 0, 3), ("E", 1, 1), ("D", 1, 2), ("C", 1, 3), ("C", 2, 2), ("E", 0, 3),
+    ("E", 1, 2), ("D", 2, 1), ("X", 0, 0), ("E", 2, 1), ("C", 2, 3), ("Q", 0, 0), ("D", 1, 3), ("X", 0, 1),
+    ("D", 2, 2), ("E", 1, 3), ("E", 2, 2), ("X", 1, 0), ("D", 2, 3), ("X", 1, 1), ("E", 2, 3), ("X", 2, 0),
+    ("X", 2, 1), ("W", 0, 0), ("W", 1, 0), ("W", 2, 0),
 )
 
 
@@ -74,6 +75,10 @@
     def came(k):
         return lax.rem(z + NT - k, NT)
 
+    first = 1 + (z // 2) * (1 - lax.rem(z, 2))
+    second = 3 - lax.rem(z, 2) * (1 - z // 2)
+    order = (0, first, second, 6 - first - second)
+
     def far_copy(k):
         return remote(far_in, far_all.at[z], far_s.at[k], far_r.at[k], {"ta": to(k)})
 
@@ -88,15 +93,15 @@
     def o_copy(j, k):
         return remote(o_out.at[j, to(k)], o_in.at[z * GROUP + j], o_s.at[j, k], o_r.at[j, k], {"ta": to(k)})
 
-    def y_copy(j, k, i):
+    def y_copy(j, r, i):
         table = tables[j]
-        base = came(k) * NH
+        base = came(order[r]) * NH
 
         def slab(row):
             return table.at[base + row]
 
         if i < 3:
-            src = kv_out.at[z * GROUP + j] if k == 0 else slab(h)
+            src = kv_out.at[z * GROUP + j] if r == 0 else slab(h)
             dst = slab(h)
             device = (h_after, h_before, h_twin)[i]
         elif i == 3:
@@ -108,7 +113,7 @@
         else:
             src = dst = slab((h_before, h_after, h_across)[i - 5])
             device = h_twin
-        return remote(src, dst, y_s.at[j, k, i], y_r.at[j, k, i], {"ha": device})
+        return remote(src, dst, y_s.at[j, r, i], y_r.at[j, r, i], {"ha": device})
 
     def own_kv(j):
         return pltpu.make_async_copy(kv_out.at[z * GROUP + j], tables[j].at[z * NH + h], own_sem.at[j, 0])
@@ -124,7 +129,22 @@
     def lanes(head):
         return pl.ds(pl.multiple_of(head * HD, HD), HD)
 
+    def pass_on(j, r):
+        for i in range(3):
+            y_copy(j, r, i).start()
+
     own_far.start()
+    def prepare_queries(j):
+        for k in range(NT):
+            head = to(k) * GROUP + j
+            for w, tile in enumerate(untile(q_in[:, :, :, lanes(head)])):
+                q_out[head, w] = tile
+        own_q(j).start()
+
+    def send_queries(j):
+        for k in range(1, NT):
+            q_copy(j, k).start()
+
     loads[0].wait()
     loads[1].wait()
     for j in range(GROUP):
@@ -137,39 +157,38 @@
             pl.semaphore_wait(barrier, len(partners))
         for k in range(1, NT):
             kv_copy(j, k).start()
-        for i in range(3):
-            y_copy(j, 0, i).start()
+        if j < GROUP - 1:
+            pass_on(j, 0)
         own_kv(j).start()
+        if j == 1:
+            loads[2].wait()
+            prepare_queries(0)
+            send_queries(0)
     for k in range(1, NT):
         far_copy(k).start()
-    loads[2].wait()
-    for j in range(GROUP):
-        for k in range(NT):
-            head = to(k) * GROUP + j
-            for w, tile in enumerate(untile(q_in[:, :, :, lanes(head)])):
-                q_out[head, w] = tile
-        own_q(j).start()
-
-    def send_queries():
-        for j in range(GROUP):
-            for k in range(1, NT):
-                q_copy(j, k).start()
+    for j in range(1, GROUP):
+        prepare_queries(j)
 
     at_end = jnp.logical_or(z == 0, z == NT - 1)
-    pl.when(jnp.logical_not(at_end))(send_queries)
-
-    def step_d(j, k):
-        y_copy(j, k, 0).wait_recv()
-        y_copy(j, k, 3).start()
-        y_copy(j, k, 5).start()
-        y_copy(j, k, 1).wait_recv()
-        y_copy(j, k, 4).start()
-        y_copy(j, k, 6).start()
-
-    def step_e(j, k):
-        y_copy(j, k, 3).wait_recv()
-        y_copy(j, k, 4).wait_recv()
-        y_copy(j, k, 7).start()
+
+    def send_rest():
+        for j in range(1, GROUP):
+            send_queries(j)
+
+    pl.when(jnp.logical_not(at_end))(send_rest)
+
+    def step_d(j, r):
+        y_copy(j, r, 0).wait_recv()
+        y_copy(j, r, 3).start()
+        y_copy(j, r, 5).start()
+        y_copy(j, r, 1).wait_recv()
+        y_copy(j, r, 4).start()
+        y_copy(j, r, 6).start()
+
+    def step_e(j, r):
+        y_copy(j, r, 3).wait_recv()
+        y_copy(j, r, 4).wait_recv()
+        y_copy(j, r, 7).start()
 
     def unit(j, t, w):
         table = tables[j]
@@ -216,18 +235,19 @@
             accum = gather(table[tile // 2, 1, lax.rem(tile, 2)], 5 * SLAB + f * TILE, accum)
         o_out[j, t, w] = (accum[:, :HD] / accum[:, HD:]).astype(jnp.bfloat16)
 
-    def attend(j):
-        if j == 0:
-            own_far.wait()
+    def attend(j, half):
+        if half == 0:
+            if j == 0:
+                own_far.wait()
+                for k in range(1, NT):
+                    far_copy(k).wait_recv()
+            own_kv(j).wait()
+            own_q(j).wait()
             for k in range(1, NT):
-                far_copy(k).wait_recv()
-        own_kv(j).wait()
-        own_q(j).wait()
-        for k in range(1, NT):
-            q_copy(j, k).wait_recv()
-        for k in range(NT):
-            for i in (2, 5, 6, 7):
-                y_copy(j, k, i).wait_recv()
+                q_copy(j, k).wait_recv()
+            for r in range(NT):
+                for i in (2, 5, 6, 7):
+                    y_copy(j, r, i).wait_recv()
 
         def queries_of(k, carry):
             t = to(k)
@@ -240,8 +260,9 @@
 
             return carry
 
-        lax.fori_loop(1, NT + 1, queries_of, 0)
-        own_o(j).start()
+        lax.fori_loop(2 * half + 1, 2 * half + 3, queries_of, 0)
+        if half:
+            own_o(j).start()
 
     def write(j, k):
         head = came(k) * GROUP + j
@@ -259,19 +280,19 @@
             )
             write(j, k).start()
 
-    for step, j, k in STEPS:
+    for step, j, r in STEPS:
         if step == "C":
-            kv_copy(j, k).wait_recv()
-            for i in range(3):
-                y_copy(j, k, i).start()
+            if r:
+                kv_copy(j, order[r]).wait_recv()
+            pass_on(j, r)
         elif step == "D":
-            step_d(j, k)
+            step_d(j, r)
         elif step == "E":
-            step_e(j, k)
+            step_e(j, r)
         elif step == "Q":
-            pl.when(at_end)(send_queries)
+            pl.when(at_end)(send_rest)
         elif step == "X":
-            attend(j)
+            attend(j, r)
         else:
             collect(j)
 

time: 154 us -> 148 us (0.961)
  Pallas kernels: 151 us -> 145 us
    pallas_call x1, Pallas kernels: 151 us -> 145 us  [body(): pl.pallas_call(kernel, out_shape=jax.ShapeDtypeStruct(queries.shape, bf),...]
where the time goes in v2:
time: 148 us; the launch traced here: 147 us
  Pallas kernels  145 us (98%)
  local copies, waits for them, and re-layouts  2.65 us (2%)
    pallas_call x1, Pallas kernels, body(): pl.pallas_call(kernel, out_shape=jax.ShapeDtypeStruct(queries.shape, bf),...  145 us

profile of v2, /device:TPU:36, one launch (start us, length us, event | category | flops | bytes accessed | tf_op | source)
XLA Modules:
  0.0 147.5 jit_solution(816857160734040593)
XLA Ops:
  0.0 144.8 %shard_map.46 = bf16[4,8,16,1536]{3,2,1,0:T(8,128)(2,1)} custom-call(bf16[4,8,16,1536]{3,2,1,0:T(8,128)(2,1)} %q_hbm.1, bf16[4,8,16,1536]{3,2,1,0:T(8,128)(2,1)} %k_hbm.1, bf16[4,8,16,1536]{3,2,1,0:T(8,128)(2,1)} %v_hbm.1, s32[2,4,12]{2,1,0:T(4,128)} %bitcast.1), custom_call_target="tpu_custom_call" | custom-call | tf_op jit(solution)/shard_map/pallas_call | solution.py:319
  144.8 2.7 %copy.6 = bf16[4,8,16,1536]{3,2,1,0:T(8,128)(2,1)} copy(bf16[4,8,16,1536]{3,2,1,0:T(8,128)(2,1)} %shard_map.46) | data formatting | bytes 3145728

commit v3 on v2

--- a/solution.py
+++ b/solution.py
@@ -25,7 +25,7 @@
     ("C", 0, 1), ("D", 0, 0), ("C", 0, 2), ("D", 1, 0), ("C", 2, 0), ("E", 0, 0), ("D", 0, 1), ("E", 1, 0),
     ("D", 0, 2), ("E", 0, 1), ("C", 1, 1), ("C", 0, 3), ("C", 1, 2), ("D", 2, 0), ("E", 0, 2), ("D", 1, 1),
     ("E", 2, 0), ("C", 2, 1), ("D", 0, 3), ("E", 1, 1), ("D", 1, 2), ("C", 1, 3), ("C", 2, 2), ("E", 0, 3),
-    ("E", 1, 2), ("D", 2, 1), ("X", 0, 0), ("E", 2, 1), ("C", 2, 3), ("Q", 0, 0), ("D", 1, 3), ("X", 0, 1),
+    ("E", 1, 2), ("D", 2, 1), ("X", 0, 0), ("E", 2, 1), ("C", 2, 3), ("D", 1, 3), ("Q", 0, 0), ("X", 0, 1),
     ("D", 2, 2), ("E", 1, 3), ("E", 2, 2), ("X", 1, 0), ("D", 2, 3), ("X", 1, 1), ("E", 2, 3), ("X", 2, 0),
     ("X", 2, 1), ("W", 0, 0), ("W", 1, 0), ("W", 2, 0),
 )

time: 148 us -> 148 us (level)
  no operation moved by 1% of the time
where the time goes in v3:
time: 148 us; the launch traced here: 147 us
  Pallas kernels  145 us (98%)
  local copies, waits for them, and re-layouts  2.65 us (2%)
    pallas_call x1, Pallas kernels, body(): pl.pallas_call(kernel, out_shape=jax.ShapeDtypeStruct(queries.shape, bf),...  145 us

profile of v3, /device:TPU:36, one launch (start us, length us, event | category | flops | bytes accessed | tf_op | source)
XLA Modules:
  0.0 147.5 jit_solution(13630049888281562545)
XLA Ops:
  0.0 144.8 %shard_map.46 = bf16[4,8,16,1536]{3,2,1,0:T(8,128)(2,1)} custom-call(bf16[4,8,16,1536]{3,2,1,0:T(8,128)(2,1)} %q_hbm.1, bf16[4,8,16,1536]{3,2,1,0:T(8,128)(2,1)} %k_hbm.1, bf16[4,8,16,1536]{3,2,1,0:T(8,128)(2,1)} %v_hbm.1, s32[2,4,12]{2,1,0:T(4,128)} %bitcast.1), custom_call_target="tpu_custom_call" | custom-call | tf_op jit(solution)/shard_map/pallas_call | solution.py:319
  144.8 2.7 %copy.6 = bf16[4,8,16,1536]{3,2,1,0:T(8,128)(2,1)} copy(bf16[4,8,16,1536]{3,2,1,0:T(8,128)(2,1)} %shard_map.46) | data formatting | bytes 3145728
